TPU v7x, 512 devices: a whole 4x8x8 slice. The times are simulated.
512 devices in a mesh: ctx: 64 (over y, z), kvh: 8 (over x, core).
Axes of the slice: x: 4, y: 8, z: 8, core: 2. Of those that a mesh axis runs over, the one named last changes fastest.
Arguments:
- queries: bfloat16 [8192, 8192], P(('ctx', 'kvh')), may hold values from -8 to 8
- keys: bfloat16 [8, 131072, 128], P('kvh', 'ctx'), may hold values from -4 to 4
- values: bfloat16 [8, 131072, 128], P('kvh', 'ctx'), may hold values from -6 to 6
- vertical: int32 [8, 8], P('kvh'), may hold values from 0 to 2047, as said below
- slash_blocks: int32 [8, 128, 32], P('kvh', 'ctx'), may hold values from 0 to 2047, as said below
- slash_count: int32 [8, 128], P('kvh', 'ctx'), may hold values from 4 to 32
- row_order: int32 [8, 128], P('kvh', 'ctx'), may hold values from 0 to 127, as said below
Outputs:
- attended: bfloat16 [8192, 8192], P(('ctx', 'kvh'))
Inputs may be any that keep to these rules, and one draw needn't show every extreme that they name: Key block k lies on ctx device k // 32; the 8 vertical blocks of a KV head lie on 8 different ctx devices. `slash_blocks`: only the first slash_count entries of a query block are used; they are distinct and none is a vertical block of the same KV head. Taking the used entries of all query blocks of a ctx device and of its partner (the device whose ctx index differs by half of the ctx axis) together, at most 2 distinct key blocks lie on any one ctx device, and this bound is reached in every draw. `row_order`: each KV head's row is a permutation of the query blocks. Output slot s lies on ctx device s // 2; of a device's 2 slots, the first 1 name query blocks of that device in increasing order, the last 1 name query blocks of its partner in increasing order.
All inputs are finite; a program needn't handle non-finite values.
Results may differ from a plain program's by a relative error of at most 0.0047.
Values may be sent and summed in bfloat16 or wider, within the bound.
A program may use at most 64 MiB of HBM per device.

v0:
```python
import math

import jax
import jax.numpy as jnp
from jax import lax
from jax.sharding import PartitionSpec as P

BLK = 64
CAP = 2
MOVE = 1


def swapped(block, axis, bit):
    count = lax.axis_size(axis)
    route = []
    for low in range(count):
        high = low | 1 << bit
        if high != low and high < count:
            route += [(low, high), (high, low)]
    return lax.ppermute(block, axis, route)


def per_device(queries, keys, values, vertical, slash_blocks, slash_count, row_order):
    ndev = lax.axis_size("ctx")
    me = lax.axis_index("ctx")
    mine = lax.all_to_all(queries, "kvh", split_axis=1, concat_axis=0, tiled=True)
    width = mine.shape[1]
    head_dim = keys.shape[2]
    groups = width // head_dim
    block_rows = slash_count.shape[1]
    kb_dev = keys.shape[1] // BLK
    key_blocks = keys[0].reshape(kb_dev, BLK, head_dim)
    value_blocks = values[0].reshape(kb_dev, BLK, head_dim)
    columns = vertical[0]
    lists = slash_blocks[0]
    counts = slash_count[0]
    order = row_order[0]
    query_blocks = mine.reshape(block_rows, BLK, width)
    staying = block_rows - MOVE
    stay_index = order[:staying] - me * block_rows
    index_row = jnp.arange(block_rows, dtype=jnp.int32)
    kept = jnp.any(index_row[:, None] == stay_index[None, :], axis=1)
    leaving = jnp.logical_not(kept).astype(jnp.int32)
    leave_rank = jnp.cumsum(leaving) - 1
    moving_slots = jnp.arange(MOVE, dtype=jnp.int32)
    leave_hit = (leaving[:, None] == 1) & (leave_rank[:, None] == moving_slots[None, :])
    sent_index = jnp.sum(jnp.where(leave_hit, index_row[:, None], 0), axis=0)
    bit = ndev.bit_length() - 2
    total_blocks = ndev * kb_dev
    block_ids = jnp.arange(total_blocks, dtype=jnp.int32)
    used = jnp.arange(lists.shape[1], dtype=jnp.int32)[None, :] < counts[:, None]
    hits = (lists[:, :, None] == block_ids[None, None, :]) & used[:, :, None]
    need = jnp.any(hits, axis=(0, 1))
    column_hits = columns[:, None] == block_ids[None, :]
    slot_count = CAP + 1
    need = need | jnp.any(column_hits, axis=0)
    need_grid = need.reshape(ndev, kb_dev).astype(jnp.int32)
    rank = jnp.cumsum(need_grid, axis=1) - 1
    slots = jnp.arange(slot_count, dtype=jnp.int32)
    match = (need_grid[:, :, None] == 1) & (rank[:, :, None] == slots[None, None, :])
    local_ids = jnp.arange(kb_dev, dtype=jnp.int32)
    wanted = jnp.sum(jnp.where(match, local_ids[None, :, None], 0), axis=1)
    wanted = jnp.where(jnp.any(match, axis=1), wanted, -1)
    asked = lax.all_to_all(wanted, "ctx", split_axis=0, concat_axis=0, tiled=True)
    valid = asked >= 0
    pick = jnp.clip(asked, 0, kb_dev - 1)
    reply_keys = jnp.where(valid[:, :, None, None], key_blocks[pick], jnp.zeros((), jnp.bfloat16))
    reply_values = jnp.where(
        valid[:, :, None, None], value_blocks[pick], jnp.zeros((), jnp.bfloat16)
    )
    got_keys, got_values = (
        lax.all_to_all(reply_keys, "ctx", split_axis=0, concat_axis=0, tiled=True),
        lax.all_to_all(reply_values, "ctx", split_axis=0, concat_axis=0, tiled=True),
    )
    got_keys = got_keys.reshape(ndev * slot_count, BLK, head_dim)
    got_values = got_values.reshape(ndev * slot_count, BLK, head_dim)
    position = (jnp.arange(ndev, dtype=jnp.int32)[:, None] * slot_count + rank).reshape(-1)
    column_position = jnp.sum(jnp.where(column_hits, position[None, :], 0), axis=1)
    column_keys = got_keys[column_position]
    column_values = got_values[column_position]
    key_pool = jnp.concatenate([column_keys, got_keys], axis=0)
    value_pool = jnp.concatenate([column_values, got_values], axis=0)
    column_count = columns.shape[0]
    slash_position = jnp.sum(jnp.where(hits, position[None, None, :], 0), axis=2) + column_count
    rows = lists.shape[0]
    entries = jnp.concatenate(
        [
            jnp.broadcast_to(
                jnp.arange(column_count, dtype=jnp.int32)[None, :], (rows, column_count)
            ),
            slash_position,
        ],
        axis=1,
    )
    span = entries.shape[1]
    live_counts = column_count + counts
    scale = 1.0 / math.sqrt(head_dim)

    def one_row(item):
        query_block, entry, live = item
        query_mat = query_block.reshape(BLK, groups, head_dim)
        key_mat = key_pool[entry].reshape(span * BLK, head_dim)
        value_mat = value_pool[entry].reshape(span * BLK, head_dim)
        scores = (
            jnp.einsum("tgd,kd->tgk", query_mat, key_mat, preferred_element_type=jnp.float32)
            * scale
        )
        alive = jnp.repeat(jnp.arange(span, dtype=jnp.int32) < live, BLK)
        scores = jnp.where(alive, scores, -jnp.inf)
        peak = jnp.max(scores, axis=-1, keepdims=True)
        weights = jnp.exp(scores - peak)
        total = jnp.sum(weights, axis=-1)
        acc = jnp.einsum(
            "tgk,kd->tgd",
            weights.astype(jnp.bfloat16),
            value_mat,
            preferred_element_type=jnp.float32,
        )
        return (acc / total[..., None]).astype(jnp.bfloat16).reshape(BLK, width)

    results = lax.map(one_row, (query_blocks, entries, live_counts))
    moved_outputs = swapped(results[sent_index], "ctx", bit)
    placed = jnp.concatenate([results[stay_index], moved_outputs], axis=0)
    placed = placed.reshape(block_rows * BLK, width)
    return lax.all_to_all(placed, "kvh", split_axis=0, concat_axis=1, tiled=True)


def solution(mesh):
    in_specs = (
        P(("ctx", "kvh"), None),
        P("kvh", "ctx", None),
        P("kvh", "ctx", None),
        P("kvh", None),
        P("kvh", "ctx", None),
        P("kvh", "ctx"),
        P("kvh", "ctx"),
    )
    out_specs = P(("ctx", "kvh"), None)
    return jax.shard_map(
        per_device, mesh=mesh, in_specs=in_specs, out_specs=out_specs, check_vma=False
    )
```

profile of v0, /device:TPU:40, one launch (start us, length us, event | category | flops | bytes accessed | tf_op | source)
XLA Modules:
  0.0 291.7 jit_solution(10488664108226130906)
XLA Ops:
  0.0 0.8 iota_compare_fusion.4
  0.8 0.8 fusion.15
  1.5 0.8 fusion.14
  2.5 0.2 reduce_window_sum.18
  3.0 0.1 copy.20
  3.1 24.1 %all_to_all.51 = s32[64,1,3]{2,1,0:T(1,128)S(1)} all-to-all(s32[64,1,3]{2,1,0:T(1,128)S(1)} %copy.20), channel_id=1, replica_groups=mesh['ctx'=64,'kvh'=8] {'ctx'}, dimensions={0} | all-to-all | bytes 1536 | tf_op jit(solution)/shard_map/all_to_all | solution.py:64
  27.2 0.1 reshape.314
  27.4 2.8 gather_fusion.2
  30.2 2.7 gather_fusion.4
  32.9 0.1 copy.21
  33.0 0.1 copy.22
  33.2 4.3 %broadcast_select_fusion = (bf16[64,3,64,128]{3,2,1,0:T(8,128)(2,1)S(1)}, bf16[64,3,64,128]{3,2,1,0:T(8,128)(2,1)}) fusion(bf16[64,3,64,128]{3,2,1,0:T(8,128)(2,1)} %bitcast.88, pred[64,3]{1,0:T(8,128)(4,1)S(1)} %copy.22, bf16[64,3,64,128]{3,2,1,0:T(8,128)(2,1)} %bitcast.87), kind=kLoop, calls=%fused_computation.24 | loop fusion | flops 3145728 | bytes 12583104 | tf_op jit(solution)/shard_map/jit(_where)/select_n | solution.py:68
  37.5 85.8 %all_to_all.52 = bf16[64,3,64,128]{3,2,1,0:T(8,128)(2,1)} all-to-all(bf16[64,3,64,128]{3,2,1,0:T(8,128)(2,1)S(1)} %get-tuple-element.85), channel_id=1, replica_groups=mesh['ctx'=64,'kvh'=8] {'ctx'}, dimensions={0} | all-to-all | bytes 6291456 | tf_op jit(solution)/shard_map/all_to_all | solution.py:73
  123.3 8.8 %all-to-all-start.2 = ((bf16[64,3,64,128]{3,2,1,0:T(8,128)(2,1)}), bf16[64,3,64,128]{3,2,1,0:T(8,128)(2,1)}, u32[]{:S(2)}, u32[]{:S(2)}) async-start(bf16[64,3,64,128]{3,2,1,0:T(8,128)(2,1)} %get-tuple-element.86), calls=%async_computation.2 | async-start | bytes 6291456 | tf_op jit(solution)/shard_map/all_to_all | solution.py:72
  132.1 0.2 reduce-window.4
  132.3 0.7 fusion.19
  134.3 0.7 copy.28
  135.7 0.3 select_reduce_fusion
  136.1 0.2 select_reduce_fusion.1
  136.3 2.5 gather_fusion.5
  138.8 85.5 %all-to-all-done.2 = bf16[64,3,64,128]{3,2,1,0:T(8,128)(2,1)} async-done(((bf16[64,3,64,128]{3,2,1,0:T(8,128)(2,1)}), bf16[64,3,64,128]{3,2,1,0:T(8,128)(2,1)}, u32[]{:S(2)}, u32[]{:S(2)}) %all-to-all-start.2) | async-done | bytes 3145760 | tf_op jit(solution)/shard_map/all_to_all | solution.py:72
  224.3 4.3 %all-to-all-start = ((bf16[16,8,1024]{2,0,1:T(8,128)(2,1)}), bf16[16,8,1024]{2,0,1:T(8,128)(2,1)S(1)}, u32[]{:S(2)}, u32[]{:S(2)}) async-start(bf16[16,8,1024]{2,0,1:T(8,128)(2,1)} %bitcast.58), calls=%async_computation | async-start | bytes 524288 | tf_op jit(solution)/shard_map/all_to_all | solution.py:26
  228.6 3.9 %pad_maximum_fusion.1 = bf16[200,64,128]{2,1,0:T(8,128)(2,1)} fusion(bf16[192,64,128]{2,1,0:T(8,128)(2,1)} %bitcast.85, bf16[8,64,128]{2,1,0:T(8,128)(2,1)S(1)} %gather_fusion.5), kind=kLoop, calls=%fused_computation.23 | loop fusion | flops 1638400 | bytes 6553600 | tf_op jit(solution)/shard_map/concatenate | solution.py:82
  232.5 2.5 gather_fusion.3
  234.9 3.9 %pad_maximum_fusion = bf16[200,64,128]{2,1,0:T(8,128)(2,1)} fusion(bf16[192,64,128]{2,1,0:T(8,128)(2,1)} %bitcast.17, bf16[8,64,128]{2,1,0:T(8,128)(2,1)S(1)} %gather_fusion.3), kind=kLoop, calls=%fused_computation.22 | loop fusion | flops 1638400 | bytes 6553600 | tf_op jit(solution)/shard_map/concatenate | solution.py:81
  238.9 28.6 %while.12 = (s32[]{:T(128)}, bf16[2,64,1024]{2,1,0:T(8,128)(2,1)S(1)}, s32[2]{0:T(128)S(1)}, bf16[2,64,1024]{2,1,0:T(8,128)(2,1)S(1)}, s32[2,40]{1,0:T(2,128)S(1...) while((s32[]{:T(128)}, bf16[2,64,1024]{2,1,0:T(8,128)(2,1)S(1)}, ...), condition=%wide.region_10.11_spmd, body=%wide.region_7.10_spmd.sunk | while | flops 680394880 | bytes 41968636 | solution.py:121
  238.9 2.6 gather_fusion.1
  241.6 0.6 dynamic_slice.25
  242.2 0.6 iota_compare_fusion.6
  242.9 0.1 reshape.357
  243.0 0.9 fusion.37
  243.9 2.3 copy-done.1
  246.2 0.8 fusion.38
  247.1 2.6 gather_fusion
  249.7 3.4 %fusion.39 = bf16[64,8,128]{2,1,0:T(8,128)(2,1)S(1)} fusion(bf16[2560,128,1]{1,0,2:T(8,128)(2,1)S(1)} %bitcast.82, f32[64,8,2560]{2,1,0:T(8,128)} %copy-done.1, f32[64,8]{1,0:T(8,128)S(1)} %get-tuple-element.133, f32[64,8]{1,0:T(8,128)S(1)} %fusion.38), kind=kOutput, calls=%fused_computation.13.clone.1 | convolution fusion | flops 338296832 | bytes 6033408 | tf_op jit(solution)/shard_map/while/body/eval_jaxpr/tgk,kd->tgd/dot_general | solution.py:113
  253.2 2.6 gather_fusion.1
  255.9 0.6 dynamic_slice.25
  256.4 0.6 iota_compare_fusion.6
  257.2 0.1 reshape.357
  257.3 0.9 fusion.37
  258.2 2.3 copy-done.1
  260.5 0.8 fusion.38
  261.4 2.6 gather_fusion
  264.0 3.4 %fusion.39 = bf16[64,8,128]{2,1,0:T(8,128)(2,1)S(1)} fusion(bf16[2560,128,1]{1,0,2:T(8,128)(2,1)S(1)} %bitcast.82, f32[64,8,2560]{2,1,0:T(8,128)} %copy-done.1, f32[64,8]{1,0:T(8,128)S(1)} %get-tuple-element.133, f32[64,8]{1,0:T(8,128)S(1)} %fusion.38), kind=kOutput, calls=%fused_computation.13.clone.1 | convolution fusion | flops 338296832 | bytes 6033408 | tf_op jit(solution)/shard_map/while/body/eval_jaxpr/tgk,kd->tgd/dot_general | solution.py:113
  267.5 1.9 collective-permute-start
  269.4 9.8 %collective-permute-done = bf16[1,64,1024]{2,1,0:T(8,128)(2,1)S(1)} collective-permute-done((bf16[1,64,1024]{2,1,0:T(8,128)(2,1)S(1)}, bf16[1,64,1024]{2,1,0:T(8,128)(2,1)S(1)}, u32[]{:S(2)}, u32[]{:S(2)}) %collective-permute-start) | collective-permute-done | bytes 131104 | tf_op jit(solution)/shard_map/ppermute | solution.py:20
  279.2 11.8 %all_to_all.53 = bf16[8,16,1024]{2,1,0:T(8,128)(2,1)S(1)} all-to-all(bf16[8,16,1024]{2,1,0:T(8,128)(2,1)S(1)} %bitcast.90), channel_id=1, replica_groups=mesh['ctx'=64,'kvh'=8] {'kvh'}, dimensions={0} | all-to-all | bytes 524288 | tf_op jit(solution)/shard_map/all_to_all | solution.py:125
  291.0 0.7 copy.26
  (56 shorter events, 1.2 us)
Async XLA Ops:
  0.0 27.4 %copy-start = (bf16[1,2048,128]{2,1,0:T(8,128)(2,1)S(1)}, bf16[1,2048,128]{2,1,0:T(8,128)(2,1)}, u32[]{:S(2)}) copy-start(bf16[1,2048,128]{2,1,0:T(8,128)(2,1)} %param.10) | copy-start | bytes 1572868
  3.1 27.1 %copy-start.2 = (bf16[1,2048,128]{2,1,0:T(8,128)(2,1)S(1)}, bf16[1,2048,128]{2,1,0:T(8,128)(2,1)}, u32[]{:S(2)}) copy-start(bf16[1,2048,128]{2,1,0:T(8,128)(2,1)} %param.11) | copy-start | bytes 1572868
  123.3 8.8 %copy-start.6 = (s32[1,2]{1,0:T(1,128)S(1)}, s32[1,2]{1,0:T(1,128)}, u32[]{:S(2)}) copy-start(s32[1,2]{1,0:T(1,128)} %param.15) | copy-start | bytes 28
  123.3 11.1 %copy-start.3 = (bf16[16,8192]{1,0:T(8,128)(2,1)S(1)}, bf16[16,8192]{1,0:T(8,128)(2,1)}, u32[]{:S(2)}) copy-start(bf16[16,8192]{1,0:T(8,128)(2,1)} %param.9) | copy-start | bytes 786436
  123.3 12.4 %copy-start.4 = (s32[1,2,32]{2,1,0:T(2,128)S(1)}, s32[1,2,32]{2,1,0:T(2,128)}, u32[]{:S(2)}) copy-start(s32[1,2,32]{2,1,0:T(2,128)} %param.13) | copy-start | bytes 772
  123.3 12.8 %copy-start.5 = (s32[1,8]{1,0:T(1,128)S(1)}, s32[1,8]{1,0:T(1,128)}, u32[]{:S(2)}) copy-start(s32[1,8]{1,0:T(1,128)} %param.12) | copy-start | bytes 100
  123.3 13.0 %copy-start.7 = (s32[1,2]{1,0:T(1,128)S(1)}, s32[1,2]{1,0:T(1,128)}, u32[]{:S(2)}) copy-start(s32[1,2]{1,0:T(1,128)} %param.14) | copy-start | bytes 28
  123.3 101.0 %all-to-all-start.2 = ((bf16[64,3,64,128]{3,2,1,0:T(8,128)(2,1)}), bf16[64,3,64,128]{3,2,1,0:T(8,128)(2,1)}, u32[]{:S(2)}, u32[]{:S(2)}) async-start(bf16[64,3,64,128]{3,2,1,0:T(8,128)(2,1)} %get-tuple-element.86), calls=%async_computation.2 | async-start | bytes 6291456 | tf_op jit(solution)/shard_map/all_to_all | solution.py:72
  224.3 14.6 %all-to-all-start = ((bf16[16,8,1024]{2,0,1:T(8,128)(2,1)}), bf16[16,8,1024]{2,0,1:T(8,128)(2,1)S(1)}, u32[]{:S(2)}, u32[]{:S(2)}) async-start(bf16[16,8,1024]{2,0,1:T(8,128)(2,1)} %bitcast.58), calls=%async_computation | async-start | bytes 524288 | tf_op jit(solution)/shard_map/all_to_all | solution.py:26
  243.9 2.3 copy-start.1
  258.2 2.3 copy-start.1
  267.5 11.7 %collective-permute-start = (bf16[1,64,1024]{2,1,0:T(8,128)(2,1)S(1)}, bf16[1,64,1024]{2,1,0:T(8,128)(2,1)S(1)}, u32[]{:S(2)}, u32[]{:S(2)}) collective-permute-start(bf16[1,64,1024]{2,1,0:T(8,128)(2,1)S(1)} %get-tuple-element.82), channel_id=1, source_target_pairs={{0,256},{256,0},{8,264},{264,8},{16,272},{272,16},{24,280},{280,24... | collective-permute-start | bytes 393224 | tf_op jit(solution)/shard_map/ppermute | solution.py:20
where the time goes:
time: 293 us; the launch traced here: 292 us
  blocking collectives  122 us (42%)
  waiting for transfers between devices  95.3 us (33%)
  local copies, waits for them, and re-layouts  29.4 us (10%)
  other arithmetic  19.4 us (7%)
  starting transfers between devices  15 us (5%)
  matrix products  8.64 us (3%)
    all_to_all x1, blocking collectives, per_device(): lax.all_to_all(reply_values, 'ctx', split_axis=0, concat_axis=0, tiled=True)  85.8 us
    all_to_all x1, waiting for transfers between devices, per_device(): lax.all_to_all(reply_keys, 'ctx', split_axis=0, concat_axis=0, tiled=True)  85.5 us
    all_to_all x1, blocking collectives, per_device(): lax.all_to_all(wanted, 'ctx', split_axis=0, concat_axis=0, tiled=True)  24.1 us
    all_to_all x1, blocking collectives, per_device(): lax.all_to_all(placed, 'kvh', split_axis=0, concat_axis=1, tiled=True)  11.8 us
    ppermute x1, waiting for transfers between devices, swapped(): return lax.ppermute(block, axis, route)  9.78 us
    all_to_all x1, starting transfers between devices, per_device(): lax.all_to_all(reply_keys, 'ctx', split_axis=0, concat_axis=0, tiled=True)  8.76 us
    dot_general x2, matrix products, one_row(): jnp.einsum('tgk,kd->tgd', weights.astype(jnp.bfloat16), value_mat, prefer...  6.77 us
  transfers between devices with their start and end apart: 3, of which 2 were waited for; matrix products, arithmetic and copies ran while one was open for 5% of the time, Pallas kernels for 0%

commit v1 on v0

v1 whole, which is shorter than its diff:
```python
import math

import jax
import jax.numpy as jnp
from jax import lax
from jax.experimental import pallas as pl
from jax.experimental.pallas import tpu as pltpu
from jax.sharding import PartitionSpec as P

MESH = pl.DeviceIdType.MESH
BLK = 64
HD = 128
QH = 8
NY = 8
NZ = 8
NCTX = NY * NZ
NKV = 8
WIDTH = QH * HD
TOK = 16
SMAX = 32
STAT = WIDTH + 128
NEG = -1e30
SCALE2 = math.log2(math.e) / math.sqrt(HD)
LOG2E = math.log2(math.e)
ROUTES = ((0, 0, 2, (0, 1)), (-1, 2, 2, (0, 1)), (1, 4, 2, (0, 1)), (-2, 6, 1, (0,)), (2, 7, 1, (1,)))
SEND_ORDER = (4, 3, 5, 2, 6, 1, 7, 0)
WORK_ORDER = (0, 4, 3, 5, 2, 6, 1, 7)


def wait_for(ref, sem):
    pltpu.make_async_copy(ref, ref, sem).wait()


def kernel(
    q_ref, k_ref, v_ref, vert_ref, lists_ref, cnt_ref, ord_ref, out_ref,
    kbuf, vbuf, mrow, mall, msm, pickv, picks, qbuf, q2, stag, kv, va, vb, vc,
    acc, mx, ls, bias, ostage, orecv,
    lsem, s_meta, s_q, s_va, s_vb, s_vc, s_kv, s_out,
    r_meta, r_q, r_va, r_vb, r_vc, r_kv, r_out,
):
    me = lax.axis_index("ctx")
    h = lax.axis_index("kvh")
    y, z = me // NZ, me % NZ

    def at(yy, zz):
        return lax.rem(yy + 2 * NY, NY) * NZ + lax.rem(zz + 2 * NZ, NZ)

    def push(src, dst, ssem, rsem, ctx, kvh):
        pltpu.make_async_remote_copy(
            src_ref=src, dst_ref=dst, send_sem=ssem, recv_sem=rsem,
            device_id=(ctx, kvh), device_id_type=MESH,
        ).start()

    load_k = pltpu.make_async_copy(k_ref, kbuf, lsem.at[0])
    load_v = pltpu.make_async_copy(v_ref, vbuf, lsem.at[1])
    load_k.start()
    load_v.start()

    homes = (at(y + 2, z), at(y - 2, z))

    barrier = pltpu.get_barrier_semaphore()

    def greet(t, _):
        pl.semaphore_signal(
            barrier, inc=1, device_id=(lax.rem(me + t, NCTX), h), device_id_type=MESH
        )
        return 0

    lax.fori_loop(1, NCTX, greet, 0)
    for home in homes:
        def greet_heads(t, _, home=home):
            pl.semaphore_signal(
                barrier, inc=1, device_id=(home, lax.rem(h + t, NKV)), device_id_type=MESH
            )
            return 0

        lax.fori_loop(1, NKV, greet_heads, 0)

    lane = lax.broadcasted_iota(jnp.int32, (1, 128), 1)
    mrow[0] = jnp.full((1, 128), -1, jnp.int32)
    mrow[0, :, 0:SMAX] = lists_ref[0, 0:1, :]
    mrow[0, :, SMAX:2 * SMAX] = lists_ref[0, 1:2, :]
    row = mrow[0]
    limit = jnp.where(lane < SMAX, cnt_ref[0, 0], cnt_ref[0, 1] + SMAX)
    row = jnp.where(lane < limit, row, -1)
    row = jnp.where(lane == 2 * SMAX, ord_ref[0, 0], row)
    row = jnp.where(lane == 2 * SMAX + 1, ord_ref[0, 1], row)
    mrow[0] = row
    mall[me] = row

    pl.semaphore_wait(barrier, NCTX - 1 + 2 * (NKV - 1))

    def send_meta(t, _):
        push(mrow.at[0], mall.at[me], s_meta, r_meta, lax.rem(me + t, NCTX), h)
        return 0

    lax.fori_loop(1, NCTX, send_meta, 0)

    token_rows = pl.ds(pl.multiple_of(lax.rem(h, 4) * TOK, TOK), TOK)
    for where in range(2):
        target = homes[1 - where]
        for t in range(NKV):
            push(
                q_ref.at[:, pl.ds(t * WIDTH, WIDTH)],
                qbuf.at[where * 2 + h // 4, token_rows, :],
                s_q, r_q, target, t,
            )

    load_k.wait()
    load_v.wait()
    mine = jnp.int32(0)
    for i in range(NKV):
        entry = vert_ref[0, i]
        mine = jnp.where(entry // 32 == me, lax.rem(entry, 32), mine)
    va[0, 0] = kbuf[mine]
    va[0, 1] = vbuf[mine]
    for a in range(1, NY):
        push(va.at[0], va.at[a], s_va, r_va, at(y + a, z), h)

    wait_for(mall.at[pl.ds(0, NCTX - 1)], r_meta)
    low = mall[0:NCTX // 2].reshape(NCTX // 2, 128)
    high = mall[NCTX // 2:NCTX].reshape(NCTX // 2, 128)
    wide = lax.broadcasted_iota(jnp.int32, (NCTX // 2, 128), 1)
    entries = jnp.where(wide < 2 * SMAX, low, pltpu.roll(high, 2 * SMAX, 1))
    own = lax.shift_right_arithmetic(entries, 5) == me
    local = entries & 31
    first = jnp.min(jnp.where(own, local, 99), axis=1, keepdims=True)
    last = jnp.max(jnp.where(own, local, 0), axis=1, keepdims=True)
    first = jnp.where(first == 99, 0, first)
    pickv[...] = jnp.where(wide == 0, first, last)
    to_picks = pltpu.make_async_copy(pickv, picks, lsem.at[2])
    to_picks.start()
    to_msm = [
        pltpu.make_async_copy(mall.at[homes[i]], msm.at[i], lsem.at[3 + i]) for i in range(2)
    ]
    for copy in to_msm:
        copy.start()
    to_picks.wait()

    for dz in SEND_ORDER:
        for dy, start, count, which in ROUTES:
            pair = lax.rem(y + dy + 2 + NY, 4) * NZ + lax.rem(z + dz, NZ)
            here = dz == 0 and dy == 0
            for i in range(count):
                pick = picks[pair, which[i]]
                if here:
                    kv[dz, start + i, 0] = kbuf[pick]
                    kv[dz, start + i, 1] = vbuf[pick]
                else:
                    stag[dz, start + i, 0] = kbuf[pick]
                    stag[dz, start + i, 1] = vbuf[pick]
            if not here:
                span = pl.ds(start, count)
                push(
                    stag.at[dz, span], kv.at[dz, span], s_kv.at[dz], r_kv.at[dz],
                    at(y + dy, z + dz), h,
                )

    owner = vert_ref[0, y] // 32
    near = lax.rem(y - owner // NZ + NY, NY)
    wait_for(va.at[pl.ds(1, NY - 1)], r_va)
    vb[0] = va[near]
    for b in range(1, NZ):
        push(vb.at[0], vb.at[b], s_vb, r_vb, at(y, z + b), h)

    for copy in to_msm:
        copy.wait()
    slot = lax.broadcasted_iota(jnp.int32, (NZ, 8 * BLK), 1) // BLK
    back = lax.broadcasted_iota(jnp.int32, (NZ, 8 * BLK), 0)
    step = jnp.where(slot < 2, 0, jnp.where(slot < 4, 1, jnp.where(slot < 6, -1, jnp.where(slot == 6, 2, -2))))
    source = ((y + step) & (NY - 1)) * NZ + ((z - back) & (NZ - 1))

    def scan(t, carry):
        lo, hi = carry
        for i in range(2):
            entry = msm[i, 0, t]
            hit = source == lax.shift_right_arithmetic(entry, 5)
            lo = jnp.where(hit, jnp.minimum(lo, entry), lo)
            hi = jnp.where(hit, jnp.maximum(hi, entry), hi)
        return lo, hi

    lo, hi = lax.fori_loop(
        0, 2 * SMAX, scan,
        (jnp.full((NZ, 8 * BLK), 1 << 20, jnp.int32), jnp.full((NZ, 8 * BLK), -3, jnp.int32)),
    )
    second = (slot == 1) | (slot == 3) | (slot == 5) | (slot == 7)
    held = jnp.where(second, jnp.where(hi > lo, hi, -2), lo)

    stay = msm[0, 0, 2 * SMAX] & 1
    came = msm[0, 0, 2 * SMAX + 1] & 1
    source_block = (stay, 2 + came, 3 - came, 1 - stay)
    for r in range(4):
        block = source_block[r]
        side = block // 2
        first_entry = lax.rem(block, 2) * SMAX

        def member(t, need, side=side, first_entry=first_entry):
            return need | (held == msm[side, 0, first_entry + t]).astype(jnp.int32)

        need = lax.fori_loop(0, SMAX, member, jnp.zeros((NZ, 8 * BLK), jnp.int32))
        bias[r] = jnp.where(need > 0, 0.0, NEG)

    wait_for(qbuf, r_q)
    for r in range(4):
        for g in range(QH):
            q2[r * 2 + g // 4, pl.ds((g % 4) * BLK, BLK), :] = qbuf[
                source_block[r], :, pl.ds(g * HD, HD)
            ]
    for i in range(8):
        acc[i] = jnp.zeros((256, HD), jnp.float32)
        ls[i] = jnp.zeros((256, 128), jnp.float32)
        mx[i] = jnp.full((256, 128), NEG, jnp.float32)

    near = lax.rem(z - lax.rem(owner, NZ) + NZ, NZ)
    wait_for(vb.at[pl.ds(1, NZ - 1)], r_vb)
    index = lax.rem(y, 4)
    vc[index] = vb[near]
    for t in range(1, 4):
        push(
            vc.at[index], vc.at[index], s_vc, r_vc,
            at((y // 4) * 4 + lax.rem(index + t, 4), z), h,
        )

    def attend(load, size, dz):
        def body(i, _):
            keys, values = load()
            scores = lax.dot_general(
                q2[i], keys, (((1,), (1,)), ((), ())), preferred_element_type=jnp.float32
            )
            if dz is not None:
                scores = scores + bias[i // 2, dz:dz + 1, :]
            old = mx[i]
            new = jnp.maximum(old, jnp.max(scores, axis=1, keepdims=True))
            shrink = jnp.exp2((old - new) * SCALE2)
            peak = new * SCALE2
            weights = jnp.exp2(scores * SCALE2 - jnp.concatenate([peak] * (size // 128), axis=1))
            total = weights[:, 0:128]
            for j in range(1, size // 128):
                total = total + weights[:, j * 128:(j + 1) * 128]
            ls[i] = ls[i] * shrink + total
            acc[i] = acc[i] * shrink + jnp.dot(
                weights.astype(jnp.bfloat16), values, preferred_element_type=jnp.float32
            )
            mx[i] = new
            return 0

        lax.fori_loop(0, 8, body, 0)

    def chunk(dz):
        def load():
            return kv[dz, :, 0].reshape(8 * BLK, HD), kv[dz, :, 1].reshape(8 * BLK, HD)

        if dz == 0:
            wait_for(kv.at[0, pl.ds(2, 6)], r_kv.at[0])
        else:
            wait_for(kv.at[dz], r_kv.at[dz])
        attend(load, 8 * BLK, dz)

    chunk(WORK_ORDER[0])
    wait_for(vc.at[pl.ds(0, 3)], r_vc)
    attend(
        lambda: (vc[:, 0].reshape(4 * BLK, HD), vc[:, 1].reshape(4 * BLK, HD)), 4 * BLK, None
    )
    for dz in WORK_ORDER[1:]:
        chunk(dz)

    lanes = lax.broadcasted_iota(jnp.int32, (BLK, 128), 1)

    def finish(r, _):
        stats = jnp.zeros((BLK, 128), jnp.float32)
        for half in range(2):
            i = r * 2 + half
            total = jnp.sum(ls[i], axis=1, keepdims=True)
            mixed = acc[i] / total
            weight = mx[i] * SCALE2 + jnp.log(total) * LOG2E
            big = weight.astype(jnp.bfloat16).astype(jnp.float32)
            rest = weight - big
            mid = rest.astype(jnp.bfloat16).astype(jnp.float32)
            tail = rest - mid
            for j in range(4):
                g = half * 4 + j
                rows = slice(j * BLK, (j + 1) * BLK)
                ostage[r, :, g * HD:(g + 1) * HD] = mixed[rows].astype(jnp.bfloat16)
                stats = jnp.where(lanes == g, big[rows], stats)
                stats = jnp.where(lanes == QH + g, mid[rows], stats)
                stats = jnp.where(lanes == 2 * QH + g, tail[rows], stats)
        ostage[r, :, WIDTH:STAT] = stats.astype(jnp.bfloat16)
        return 0

    lax.fori_loop(0, 4, finish, 0)
    for i in range(2):
        for t in range(NKV):
            push(
                ostage.at[i * 2 + t // 4, pl.ds((t % 4) * TOK, TOK), :],
                orecv.at[i, h], s_out, r_out, homes[i], t,
            )

    wait_for(orecv, r_out)
    for head in range(NKV):
        logs = []
        for i in range(2):
            terms = orecv[i, head, :, WIDTH:STAT].astype(jnp.float32)
            logs.append(terms + pltpu.roll(terms, 128 - QH, 1) + pltpu.roll(terms, 128 - 2 * QH, 1))
        share = 1.0 / (1.0 + jnp.exp2(logs[1] - logs[0]))
        for g in range(QH):
            cols = slice(g * HD, (g + 1) * HD)
            part = share[:, g:g + 1]
            one = orecv[0, head, :, cols].astype(jnp.float32)
            two = orecv[1, head, :, cols].astype(jnp.float32)
            out_ref[:, head * WIDTH + g * HD:head * WIDTH + (g + 1) * HD] = (
                one * part + two * (1.0 - part)
            ).astype(jnp.bfloat16)

    wait_for(mall.at[pl.ds(0, NCTX - 1)], s_meta)
    wait_for(qbuf, s_q)
    wait_for(va.at[pl.ds(1, NY - 1)], s_va)
    wait_for(vb.at[pl.ds(1, NZ - 1)], s_vb)
    wait_for(vc.at[pl.ds(0, 3)], s_vc)
    wait_for(stag.at[0, pl.ds(2, 6)], s_kv.at[0])
    for dz in range(1, NZ):
        wait_for(stag.at[dz], s_kv.at[dz])
    wait_for(ostage, s_out)


def per_device(queries, keys, values, vertical, slash_blocks, slash_count, row_order):
    bf16, f32, i32 = jnp.bfloat16, jnp.float32, jnp.int32
    blocks = keys.shape[1] // BLK
    vmem = pltpu.VMEM
    dma = pltpu.SemaphoreType.DMA
    any_spec = pl.BlockSpec(memory_space=pl.ANY)
    vmem_spec = pl.BlockSpec(memory_space=pltpu.VMEM)
    smem_spec = pl.BlockSpec(memory_space=pltpu.SMEM)
    return pl.pallas_call(
        kernel,
        out_shape=jax.ShapeDtypeStruct(queries.shape, bf16),
        in_specs=[any_spec, any_spec, any_spec, smem_spec, vmem_spec, smem_spec, smem_spec],
        out_specs=vmem_spec,
        scratch_shapes=[
            vmem((blocks, BLK, HD), bf16),
            vmem((blocks, BLK, HD), bf16),
            vmem((1, 1, 128), i32),
            vmem((NCTX, 1, 128), i32),
            pltpu.SMEM((2, 1, 128), i32),
            vmem((NCTX // 2, 128), i32),
            pltpu.SMEM((NCTX // 2, 128), i32),
            vmem((4, BLK, WIDTH), bf16),
            vmem((8, 256, HD), bf16),
            vmem((NZ, 8, 2, BLK, HD), bf16),
            vmem((NZ, 8, 2, BLK, HD), bf16),
            vmem((NY, 2, BLK, HD), bf16),
            vmem((NZ, 2, BLK, HD), bf16),
            vmem((4, 2, BLK, HD), bf16),
            vmem((8, 256, HD), f32),
            vmem((8, 256, 128), f32),
            vmem((8, 256, 128), f32),
            vmem((4, NZ, 8 * BLK), f32),
            vmem((4, BLK, STAT), bf16),
            vmem((2, NKV, TOK, STAT), bf16),
            dma((5,)),
            dma, dma, dma, dma, dma, dma((NZ,)), dma,
            dma, dma, dma, dma, dma, dma((NZ,)), dma,
        ],
        compiler_params=pltpu.CompilerParams(
            collective_id=0, has_side_effects=True, vmem_limit_bytes=48 * 1024 * 1024
        ),
    )(
        queries,
        keys.reshape(blocks, BLK, HD),
        values.reshape(blocks, BLK, HD),
        vertical, slash_blocks, slash_count, row_order,
    )


def solution(mesh):
    in_specs = (
        P(("ctx", "kvh"), None),
        P("kvh", "ctx", None),
        P("kvh", "ctx", None),
        P("kvh", None),
        P("kvh", "ctx", None),
        P("kvh", "ctx"),
        P("kvh", "ctx"),
    )
    out_specs = P(("ctx", "kvh"), None)
    return jax.shard_map(
        per_device, mesh=mesh, in_specs=in_specs, out_specs=out_specs, check_vma=False
    )
```

time: 293 us -> 171 us (0.58)
  the two profiles are of different devices: /device:TPU:40 before, /device:TPU:15 now
where the time goes in v1:
time: 171 us; the launch traced here: 170 us
  Pallas kernels  166 us (97%)
  local copies, waits for them, and re-layouts  4.44 us (3%)
    pallas_call x1, Pallas kernels, per_device(): pl.pallas_call(kernel, out_shape=jax.ShapeDtypeStruct(queries.shape, bf16...  166 us
    unnamed x15, local copies, waits for them, and re-layouts  4.44 us

profile of v1, /device:TPU:15, one launch (start us, length us, event | category | flops | bytes accessed | tf_op | source)
XLA Modules:
  0.0 170.4 jit_solution(11656715853748628239)
XLA Ops:
  0.0 0.0 copy-start.5
  0.0 0.0 copy-start.6
  0.0 0.0 copy-start.3
  0.0 0.0 copy-start.4
  0.0 0.6 copy-done.5
  0.7 0.0 copy-done.6
  0.7 0.0 copy-done.3
  0.7 0.0 copy-done.4
  0.7 0.0 copy-start
  0.7 1.0 copy-done
  1.8 0.0 copy-start.1
  1.8 1.0 copy-done.1
  2.8 0.0 copy-start.2
  2.8 0.9 copy-done.2
  3.7 165.9 %shard_map.73 = bf16[16,8192]{1,0:T(8,128)(2,1)S(1)} custom-call(bf16[16,8192]{1,0:T(8,128)(2,1)S(1)} %copy-done.2, bf16[32,64,128]{2,1,0:T(8,128)(2,1)S(1)} %bitcast.2, bf16[32,64,128]{2,1,0:T(8,128)(2,1)S(1)} %bitcast.3, s32[1,8]{1,0:T(1,128)S(1)} %copy-done.4, s32[1,2,32]{2,1,0:T(2,128)S(1)} %copy-done.3, s32[1,2]{1,0:T(1,128)S(1)} %copy-done.5, ...), custom_call_target="tpu_custom_call" | custom-call | tf_op jit(solution)/shard_map/pallas_call | solution.py:333
  169.7 0.7 copy.9
Async XLA Ops:
  0.0 0.7 copy-start.5
  0.0 0.7 copy-start.6
  0.0 0.7 copy-start.3
  0.0 0.7 copy-start.4
  0.7 1.0 copy-start
  1.8 1.0 copy-start.1
  2.8 0.9 copy-start.2

commit v2 on v1

--- a/solution.py
+++ b/solution.py
@@ -23,8 +23,6 @@
 SCALE2 = math.log2(math.e) / math.sqrt(HD)
 LOG2E = math.log2(math.e)
 ROUTES = ((0, 0, 2, (0, 1)), (-1, 2, 2, (0, 1)), (1, 4, 2, (0, 1)), (-2, 6, 1, (0,)), (2, 7, 1, (1,)))
-SEND_ORDER = (4, 3, 5, 2, 6, 1, 7, 0)
-WORK_ORDER = (0, 4, 3, 5, 2, 6, 1, 7)
 
 
 def wait_for(ref, sem):
@@ -33,10 +31,10 @@
 
 def kernel(
     q_ref, k_ref, v_ref, vert_ref, lists_ref, cnt_ref, ord_ref, out_ref,
-    kbuf, vbuf, mrow, mall, msm, pickv, picks, qbuf, q2, stag, kv, va, vb, vc,
+    kbuf, vbuf, mrow, mall, msm, pickv, picks, qbuf, q2, gath, stag, kv, va, vb, vc,
     acc, mx, ls, bias, ostage, orecv,
-    lsem, s_meta, s_q, s_va, s_vb, s_vc, s_kv, s_out,
-    r_meta, r_q, r_va, r_vb, r_vc, r_kv, r_out,
+    lsem, s_meta, s_q, s_va, s_vb, s_vc, s_y, s_z, s_out,
+    r_meta, r_q, r_va, r_vb, r_vc, r_y, r_z, r_out,
 ):
     me = lax.axis_index("ctx")
     h = lax.axis_index("kvh")
@@ -59,22 +57,15 @@
     homes = (at(y + 2, z), at(y - 2, z))
 
     barrier = pltpu.get_barrier_semaphore()
-
-    def greet(t, _):
-        pl.semaphore_signal(
-            barrier, inc=1, device_id=(lax.rem(me + t, NCTX), h), device_id_type=MESH
-        )
-        return 0
-
-    lax.fori_loop(1, NCTX, greet, 0)
+    for t in range(1, NZ):
+        pl.semaphore_signal(barrier, inc=1, device_id=(at(y, z + t), h), device_id_type=MESH)
+    for t in range(1, NY):
+        pl.semaphore_signal(barrier, inc=1, device_id=(at(y + t, z), h), device_id_type=MESH)
     for home in homes:
-        def greet_heads(t, _, home=home):
+        for t in range(1, NKV):
             pl.semaphore_signal(
                 barrier, inc=1, device_id=(home, lax.rem(h + t, NKV)), device_id_type=MESH
             )
-            return 0
-
-        lax.fori_loop(1, NKV, greet_heads, 0)
 
     lane = lax.broadcasted_iota(jnp.int32, (1, 128), 1)
     mrow[0] = jnp.full((1, 128), -1, jnp.int32)
@@ -85,26 +76,29 @@
     row = jnp.where(lane < limit, row, -1)
     row = jnp.where(lane == 2 * SMAX, ord_ref[0, 0], row)
     row = jnp.where(lane == 2 * SMAX + 1, ord_ref[0, 1], row)
-    mrow[0] = row
     mall[me] = row
 
-    pl.semaphore_wait(barrier, NCTX - 1 + 2 * (NKV - 1))
-
-    def send_meta(t, _):
-        push(mrow.at[0], mall.at[me], s_meta, r_meta, lax.rem(me + t, NCTX), h)
-        return 0
-
-    lax.fori_loop(1, NCTX, send_meta, 0)
+    pl.semaphore_wait(barrier, NZ - 1 + NY - 1 + 2 * (NKV - 1))
+
+    for t in range(1, NZ):
+        push(mall.at[me], mall.at[me], s_meta.at[0], r_meta.at[0], at(y, z + t), h)
 
     token_rows = pl.ds(pl.multiple_of(lax.rem(h, 4) * TOK, TOK), TOK)
-    for where in range(2):
-        target = homes[1 - where]
+
+    def send_queries(where):
         for t in range(NKV):
             push(
                 q_ref.at[:, pl.ds(t * WIDTH, WIDTH)],
                 qbuf.at[where * 2 + h // 4, token_rows, :],
-                s_q, r_q, target, t,
+                s_q.at[where], r_q.at[where], homes[1 - where], t,
             )
+
+    wait_for(mall.at[pl.ds(0, NZ - 1)], r_meta.at[0])
+    my_row = pl.ds(pl.multiple_of(y * NZ, NZ), NZ)
+    for t in range(1, NY):
+        push(mall.at[my_row], mall.at[my_row], s_meta.at[1], r_meta.at[1], at(y + t, z), h)
+
+    send_queries(0)
 
     load_k.wait()
     load_v.wait()
@@ -114,10 +108,13 @@
         mine = jnp.where(entry // 32 == me, lax.rem(entry, 32), mine)
     va[0, 0] = kbuf[mine]
     va[0, 1] = vbuf[mine]
-    for a in range(1, NY):
-        push(va.at[0], va.at[a], s_va, r_va, at(y + a, z), h)
-
-    wait_for(mall.at[pl.ds(0, NCTX - 1)], r_meta)
+
+    wait_for(mall.at[pl.ds(0, NCTX - NZ)], r_meta.at[1])
+    to_msm = [
+        pltpu.make_async_copy(mall.at[homes[i]], msm.at[i], lsem.at[3 + i]) for i in range(2)
+    ]
+    for copy in to_msm:
+        copy.start()
     low = mall[0:NCTX // 2].reshape(NCTX // 2, 128)
     high = mall[NCTX // 2:NCTX].reshape(NCTX // 2, 128)
     wide = lax.broadcasted_iota(jnp.int32, (NCTX // 2, 128), 1)
@@ -130,38 +127,42 @@
     pickv[...] = jnp.where(wide == 0, first, last)
     to_picks = pltpu.make_async_copy(pickv, picks, lsem.at[2])
     to_picks.start()
-    to_msm = [
-        pltpu.make_async_copy(mall.at[homes[i]], msm.at[i], lsem.at[3 + i]) for i in range(2)
-    ]
-    for copy in to_msm:
-        copy.start()
     to_picks.wait()
 
-    for dz in SEND_ORDER:
+    def send_y(dz):
         for dy, start, count, which in ROUTES:
             pair = lax.rem(y + dy + 2 + NY, 4) * NZ + lax.rem(z + dz, NZ)
-            here = dz == 0 and dy == 0
             for i in range(count):
                 pick = picks[pair, which[i]]
-                if here:
-                    kv[dz, start + i, 0] = kbuf[pick]
-                    kv[dz, start + i, 1] = vbuf[pick]
-                else:
+                if dy == 0:
                     stag[dz, start + i, 0] = kbuf[pick]
                     stag[dz, start + i, 1] = vbuf[pick]
-            if not here:
-                span = pl.ds(start, count)
+                else:
+                    gath[dz, start + i - 2, 0] = kbuf[pick]
+                    gath[dz, start + i - 2, 1] = vbuf[pick]
+            if dy != 0:
                 push(
-                    stag.at[dz, span], kv.at[dz, span], s_kv.at[dz], r_kv.at[dz],
-                    at(y + dy, z + dz), h,
+                    gath.at[dz, pl.ds(start - 2, count)], stag.at[dz, pl.ds(start, count)],
+                    s_y.at[dz], r_y.at[dz], at(y + dy, z), h,
                 )
 
-    owner = vert_ref[0, y] // 32
-    near = lax.rem(y - owner // NZ + NY, NY)
-    wait_for(va.at[pl.ds(1, NY - 1)], r_va)
-    vb[0] = va[near]
-    for b in range(1, NZ):
-        push(vb.at[0], vb.at[b], s_vb, r_vb, at(y, z + b), h)
+    def send_z(dz):
+        wait_for(stag.at[dz, pl.ds(2, 6)], r_y.at[dz])
+        push(stag.at[dz], kv.at[dz], s_z.at[dz], r_z.at[dz], at(y, z + dz), h)
+
+    send_y(1)
+    send_y(7)
+    send_y(2)
+    send_y(6)
+    send_queries(1)
+    send_z(1)
+    send_z(7)
+    for a in range(1, NY):
+        push(va.at[0], va.at[a], s_va, r_va, at(y + a, z), h)
+    send_y(3)
+    send_y(5)
+    send_y(4)
+    send_y(0)
 
     for copy in to_msm:
         copy.wait()
@@ -200,16 +201,81 @@
         need = lax.fori_loop(0, SMAX, member, jnp.zeros((NZ, 8 * BLK), jnp.int32))
         bias[r] = jnp.where(need > 0, 0.0, NEG)
 
-    wait_for(qbuf, r_q)
+    send_z(2)
+    send_z(6)
+
+    for i in range(8):
+        acc[i] = jnp.zeros((256, HD), jnp.float32)
+        ls[i] = jnp.zeros((256, 128), jnp.float32)
+        mx[i] = jnp.full((256, 128), NEG, jnp.float32)
+
+    owner = vert_ref[0, y] // 32
+    near = lax.rem(y - owner // NZ + NY, NY)
+    wait_for(va.at[pl.ds(1, NY - 1)], r_va)
+    vb[0] = va[near]
+    for b in range(1, NZ):
+        push(vb.at[0], vb.at[b], s_vb, r_vb, at(y, z + b), h)
+
+    for where in range(2):
+        wait_for(qbuf.at[pl.ds(where * 2, 2)], r_q.at[where])
     for r in range(4):
         for g in range(QH):
             q2[r * 2 + g // 4, pl.ds((g % 4) * BLK, BLK), :] = qbuf[
                 source_block[r], :, pl.ds(g * HD, HD)
             ]
-    for i in range(8):
-        acc[i] = jnp.zeros((256, HD), jnp.float32)
-        ls[i] = jnp.zeros((256, 128), jnp.float32)
-        mx[i] = jnp.full((256, 128), NEG, jnp.float32)
+
+    send_z(3)
+    send_z(5)
+
+    def attend_rows(r, load, size, dz):
+        tiles = (2 * r, 2 * r + 1)
+        keys, values = load()
+        scores = [
+            lax.dot_general(
+                q2[i], keys, (((1,), (1,)), ((), ())), preferred_element_type=jnp.float32
+            )
+            for i in tiles
+        ]
+        if dz is not None:
+            extra = bias[r, dz:dz + 1, :]
+            scores = [s + extra for s in scores]
+        old = [mx[i] for i in tiles]
+        new = [jnp.maximum(o, jnp.max(s, axis=1, keepdims=True)) for o, s in zip(old, scores)]
+        shrink = [jnp.exp2((o - n) * SCALE2) for o, n in zip(old, new)]
+        weights = [
+            jnp.exp2(s * SCALE2 - jnp.concatenate([n * SCALE2] * (size // 128), axis=1))
+            for s, n in zip(scores, new)
+        ]
+        for k, i in enumerate(tiles):
+            total = weights[k][:, 0:128]
+            for j in range(1, size // 128):
+                total = total + weights[k][:, j * 128:(j + 1) * 128]
+            ls[i] = ls[i] * shrink[k] + total
+            acc[i] = acc[i] * shrink[k] + jnp.dot(
+                weights[k].astype(jnp.bfloat16), values, preferred_element_type=jnp.float32
+            )
+            mx[i] = new[k]
+
+    def attend(load, size, dz):
+        def body(r, _):
+            attend_rows(r, load, size, dz)
+            return 0
+
+        lax.fori_loop(0, 4, body, 0)
+
+    def chunk(dz):
+        buf = stag if dz == 0 else kv
+
+        def load():
+            return buf[dz, :, 0].reshape(8 * BLK, HD), buf[dz, :, 1].reshape(8 * BLK, HD)
+
+        if dz == 0:
+            wait_for(stag.at[0, pl.ds(2, 6)], r_y.at[0])
+        else:
+            wait_for(kv.at[dz], r_z.at[dz])
+        return load, 8 * BLK, dz
+
+    attend(*chunk(1))
 
     near = lax.rem(z - lax.rem(owner, NZ) + NZ, NZ)
     wait_for(vb.at[pl.ds(1, NZ - 1)], r_vb)
@@ -220,53 +286,23 @@
             vc.at[index], vc.at[index], s_vc, r_vc,
             at((y // 4) * 4 + lax.rem(index + t, 4), z), h,
         )
-
-    def attend(load, size, dz):
-        def body(i, _):
-            keys, values = load()
-            scores = lax.dot_general(
-                q2[i], keys, (((1,), (1,)), ((), ())), preferred_element_type=jnp.float32
-            )
-            if dz is not None:
-                scores = scores + bias[i // 2, dz:dz + 1, :]
-            old = mx[i]
-            new = jnp.maximum(old, jnp.max(scores, axis=1, keepdims=True))
-            shrink = jnp.exp2((old - new) * SCALE2)
-            peak = new * SCALE2
-            weights = jnp.exp2(scores * SCALE2 - jnp.concatenate([peak] * (size // 128), axis=1))
-            total = weights[:, 0:128]
-            for j in range(1, size // 128):
-                total = total + weights[:, j * 128:(j + 1) * 128]
-            ls[i] = ls[i] * shrink + total
-            acc[i] = acc[i] * shrink + jnp.dot(
-                weights.astype(jnp.bfloat16), values, preferred_element_type=jnp.float32
-            )
-            mx[i] = new
-            return 0
-
-        lax.fori_loop(0, 8, body, 0)
-
-    def chunk(dz):
-        def load():
-            return kv[dz, :, 0].reshape(8 * BLK, HD), kv[dz, :, 1].reshape(8 * BLK, HD)
-
-        if dz == 0:
-            wait_for(kv.at[0, pl.ds(2, 6)], r_kv.at[0])
-        else:
-            wait_for(kv.at[dz], r_kv.at[dz])
-        attend(load, 8 * BLK, dz)
-
-    chunk(WORK_ORDER[0])
+    send_z(4)
+
+    attend(*chunk(7))
+    attend(*chunk(0))
+    attend(*chunk(2))
+    attend(*chunk(6))
     wait_for(vc.at[pl.ds(0, 3)], r_vc)
     attend(
         lambda: (vc[:, 0].reshape(4 * BLK, HD), vc[:, 1].reshape(4 * BLK, HD)), 4 * BLK, None
     )
-    for dz in WORK_ORDER[1:]:
-        chunk(dz)
+    attend(*chunk(3))
+    attend(*chunk(5))
+    last_chunk = chunk(4)
 
     lanes = lax.broadcasted_iota(jnp.int32, (BLK, 128), 1)
 
-    def finish(r, _):
+    def finish(r):
         stats = jnp.zeros((BLK, 128), jnp.float32)
         for half in range(2):
             i = r * 2 + half
@@ -285,18 +321,18 @@
                 stats = jnp.where(lanes == QH + g, mid[rows], stats)
                 stats = jnp.where(lanes == 2 * QH + g, tail[rows], stats)
         ostage[r, :, WIDTH:STAT] = stats.astype(jnp.bfloat16)
-        return 0
-
-    lax.fori_loop(0, 4, finish, 0)
-    for i in range(2):
-        for t in range(NKV):
+
+    for r in (0, 2, 1, 3):
+        attend_rows(r, *last_chunk)
+        finish(r)
+        for t in range(4):
             push(
-                ostage.at[i * 2 + t // 4, pl.ds((t % 4) * TOK, TOK), :],
-                orecv.at[i, h], s_out, r_out, homes[i], t,
+                ostage.at[r, pl.ds(t * TOK, TOK), :], orecv.at[r // 2, h],
+                s_out, r_out.at[h], homes[r // 2], (r % 2) * 4 + t,
             )
 
-    wait_for(orecv, r_out)
     for head in range(NKV):
+        wait_for(orecv.at[:, head], r_out.at[head])
         logs = []
         for i in range(2):
             terms = orecv[i, head, :, WIDTH:STAT].astype(jnp.float32)
@@ -311,14 +347,17 @@
                 one * part + two * (1.0 - part)
             ).astype(jnp.bfloat16)
 
-    wait_for(mall.at[pl.ds(0, NCTX - 1)], s_meta)
-    wait_for(qbuf, s_q)
+    wait_for(mall.at[pl.ds(0, NZ - 1)], s_meta.at[0])
+    wait_for(mall.at[pl.ds(0, NCTX - NZ)], s_meta.at[1])
+    for where in range(2):
+        wait_for(qbuf.at[pl.ds(where * 2, 2)], s_q.at[where])
     wait_for(va.at[pl.ds(1, NY - 1)], s_va)
     wait_for(vb.at[pl.ds(1, NZ - 1)], s_vb)
     wait_for(vc.at[pl.ds(0, 3)], s_vc)
-    wait_for(stag.at[0, pl.ds(2, 6)], s_kv.at[0])
+    for dz in range(NZ):
+        wait_for(gath.at[dz], s_y.at[dz])
     for dz in range(1, NZ):
-        wait_for(stag.at[dz], s_kv.at[dz])
+        wait_for(stag.at[dz], s_z.at[dz])
     wait_for(ostage, s_out)
 
 
@@ -327,13 +366,13 @@
     blocks = keys.shape[1] // BLK
     vmem = pltpu.VMEM
     dma = pltpu.SemaphoreType.DMA
-    any_spec = pl.BlockSpec(memory_space=pl.ANY)
+    hbm_spec = pl.BlockSpec(memory_space=pltpu.HBM)
     vmem_spec = pl.BlockSpec(memory_space=pltpu.VMEM)
     smem_spec = pl.BlockSpec(memory_space=pltpu.SMEM)
     return pl.pallas_call(
         kernel,
         out_shape=jax.ShapeDtypeStruct(queries.shape, bf16),
-        in_specs=[any_spec, any_spec, any_spec, smem_spec, vmem_spec, smem_spec, smem_spec],
+        in_specs=[hbm_spec, hbm_spec, hbm_spec, smem_spec, vmem_spec, smem_spec, smem_spec],
         out_specs=vmem_spec,
         scratch_shapes=[
             vmem((blocks, BLK, HD), bf16),
@@ -345,6 +384,7 @@
             pltpu.SMEM((NCTX // 2, 128), i32),
             vmem((4, BLK, WIDTH), bf16),
             vmem((8, 256, HD), bf16),
+            vmem((NZ, 6, 2, BLK, HD), bf16),
             vmem((NZ, 8, 2, BLK, HD), bf16),
             vmem((NZ, 8, 2, BLK, HD), bf16),
             vmem((NY, 2, BLK, HD), bf16),
@@ -357,11 +397,11 @@
             vmem((4, BLK, STAT), bf16),
             vmem((2, NKV, TOK, STAT), bf16),
             dma((5,)),
-            dma, dma, dma, dma, dma, dma((NZ,)), dma,
-            dma, dma, dma, dma, dma, dma((NZ,)), dma,
+            dma((2,)), dma((2,)), dma, dma, dma, dma((NZ,)), dma((NZ,)), dma,
+            dma((2,)), dma((2,)), dma, dma, dma, dma((NZ,)), dma((NZ,)), dma((NKV,)),
         ],
         compiler_params=pltpu.CompilerParams(
-            collective_id=0, has_side_effects=True, vmem_limit_bytes=48 * 1024 * 1024
+            collective_id=0, has_side_effects=True, vmem_limit_bytes=60 * 1024 * 1024
         ),
     )(
         queries,

time: 171 us -> 111 us (0.65)
  the two profiles are of different devices: /device:TPU:15 before, /device:TPU:87 now
where the time goes in v2:
time: 111 us
  Pallas kernels  109 us (98%)
  local copies, waits for them, and re-layouts  1.67 us (2%)
    pallas_call x1, Pallas kernels, per_device(): pl.pallas_call(kernel, out_shape=jax.ShapeDtypeStruct(queries.shape, bf16...  109 us

profile of v2, /device:TPU:87, one launch (start us, length us, event | category | flops | bytes accessed | tf_op | source)
XLA Modules:
  0.0 110.6 jit_solution(13570316834141765795)
XLA Ops:
  0.0 109.0 %shard_map.73 = bf16[16,8192]{1,0:T(8,128)(2,1)} custom-call(bf16[16,8192]{1,0:T(8,128)(2,1)} %q_ref.1, bf16[32,64,128]{2,1,0:T(8,128)(2,1)} %bitcast.2, bf16[32,64,128]{2,1,0:T(8,128)(2,1)} %bitcast.3, s32[1,8]{1,0:T(1,128)} %vert_ref.1, s32[1,2,32]{2,1,0:T(2,128)} %lists_ref.1, s32[1,2]{1,0:T(1,128)} %cnt_ref.1, s32[1,2]{1,0:T(1,128)} %ord_ref.1), custom_call_target="tpu_custom_call" | custom-call | tf_op jit(solution)/shard_map/pallas_call | solution.py:372
  109.0 1.7 %copy.9 = bf16[16,8192]{1,0:T(8,128)(2,1)} copy(bf16[16,8192]{1,0:T(8,128)(2,1)} %shard_map.73) | data formatting | bytes 524288

commit v3 on v2

--- a/solution.py
+++ b/solution.py
@@ -18,7 +18,6 @@
 WIDTH = QH * HD
 TOK = 16
 SMAX = 32
-STAT = WIDTH + 128
 NEG = -1e30
 SCALE2 = math.log2(math.e) / math.sqrt(HD)
 LOG2E = math.log2(math.e)
@@ -31,10 +30,10 @@
 
 def kernel(
     q_ref, k_ref, v_ref, vert_ref, lists_ref, cnt_ref, ord_ref, out_ref,
-    kbuf, vbuf, mrow, mall, msm, pickv, picks, qbuf, q2, gath, stag, kv, va, vb, vc,
-    acc, mx, ls, bias, ostage, orecv,
-    lsem, s_meta, s_q, s_va, s_vb, s_vc, s_y, s_z, s_out,
-    r_meta, r_q, r_va, r_vb, r_vc, r_y, r_z, r_out,
+    kbuf, vbuf, mrow, mall, msm, pickv, picks, qbuf, q2, gath, stag, kv, va, vb, vsrc, vc,
+    acc, mx, ls, bias, ostage, orecv, lstage, lrecv,
+    lsem, s_meta, s_q, s_va, s_vb, s_vc, s_y, s_z, s_out, s_stat,
+    r_meta, r_q, r_va, r_vb, r_vc, r_y, r_z, r_out, r_stat,
 ):
     me = lax.axis_index("ctx")
     h = lax.axis_index("kvh")
@@ -86,9 +85,10 @@
     token_rows = pl.ds(pl.multiple_of(lax.rem(h, 4) * TOK, TOK), TOK)
 
     def send_queries(where):
-        for t in range(NKV):
+        for i in range(NKV):
+            t = lax.rem(h + i, NKV)
             push(
-                q_ref.at[:, pl.ds(t * WIDTH, WIDTH)],
+                q_ref.at[:, pl.ds(pl.multiple_of(t * WIDTH, WIDTH), WIDTH)],
                 qbuf.at[where * 2 + h // 4, token_rows, :],
                 s_q.at[where], r_q.at[where], homes[1 - where], t,
             )
@@ -97,8 +97,6 @@
     my_row = pl.ds(pl.multiple_of(y * NZ, NZ), NZ)
     for t in range(1, NY):
         push(mall.at[my_row], mall.at[my_row], s_meta.at[1], r_meta.at[1], at(y + t, z), h)
-
-    send_queries(0)
 
     load_k.wait()
     load_v.wait()
@@ -108,6 +106,8 @@
         mine = jnp.where(entry // 32 == me, lax.rem(entry, 32), mine)
     va[0, 0] = kbuf[mine]
     va[0, 1] = vbuf[mine]
+    for b in range(1, NZ):
+        push(va.at[0], va.at[b], s_va, r_va, at(y, z + b), h)
 
     wait_for(mall.at[pl.ds(0, NCTX - NZ)], r_meta.at[1])
     to_msm = [
@@ -140,6 +140,11 @@
                 else:
                     gath[dz, start + i - 2, 0] = kbuf[pick]
                     gath[dz, start + i - 2, 1] = vbuf[pick]
+            if dy == 0 and dz != 0:
+                push(
+                    stag.at[dz, pl.ds(0, 2)], kv.at[dz, pl.ds(0, 2)],
+                    s_z.at[dz], r_z.at[dz], at(y, z + dz), h,
+                )
             if dy != 0:
                 push(
                     gath.at[dz, pl.ds(start - 2, count)], stag.at[dz, pl.ds(start, count)],
@@ -148,21 +153,28 @@
 
     def send_z(dz):
         wait_for(stag.at[dz, pl.ds(2, 6)], r_y.at[dz])
-        push(stag.at[dz], kv.at[dz], s_z.at[dz], r_z.at[dz], at(y, z + dz), h)
-
-    send_y(1)
-    send_y(7)
-    send_y(2)
-    send_y(6)
+        push(
+            stag.at[dz, pl.ds(2, 6)], kv.at[dz, pl.ds(2, 6)],
+            s_z.at[dz], r_z.at[dz], at(y, z + dz), h,
+        )
+
+    for dz in (4, 3, 5):
+        send_y(dz)
+    send_queries(0)
     send_queries(1)
-    send_z(1)
-    send_z(7)
+    for dz in (2, 6):
+        send_y(dz)
+    for dz in (4, 3, 5):
+        send_z(dz)
+
+    owner = vert_ref[0, z] // 32
+    wait_for(va.at[pl.ds(1, NZ - 1)], r_va)
+    vb[0] = va[lax.rem(z - lax.rem(owner, NZ) + NZ, NZ)]
     for a in range(1, NY):
-        push(va.at[0], va.at[a], s_va, r_va, at(y + a, z), h)
-    send_y(3)
-    send_y(5)
-    send_y(4)
-    send_y(0)
+        push(vb.at[0], vb.at[a], s_vb, r_vb, at(y + a, z), h)
+
+    for dz in (1, 7, 0):
+        send_y(dz)
 
     for copy in to_msm:
         copy.wait()
@@ -201,20 +213,29 @@
         need = lax.fori_loop(0, SMAX, member, jnp.zeros((NZ, 8 * BLK), jnp.int32))
         bias[r] = jnp.where(need > 0, 0.0, NEG)
 
-    send_z(2)
-    send_z(6)
-
     for i in range(8):
         acc[i] = jnp.zeros((256, HD), jnp.float32)
         ls[i] = jnp.zeros((256, 128), jnp.float32)
         mx[i] = jnp.full((256, 128), NEG, jnp.float32)
 
-    owner = vert_ref[0, y] // 32
-    near = lax.rem(y - owner // NZ + NY, NY)
-    wait_for(va.at[pl.ds(1, NY - 1)], r_va)
-    vb[0] = va[near]
-    for b in range(1, NZ):
-        push(vb.at[0], vb.at[b], s_vb, r_vb, at(y, z + b), h)
+    send_z(2)
+    send_z(6)
+
+    upper = y // 4
+    wait_for(vb.at[pl.ds(1, NY - 1)], r_vb)
+    vsrc[...] = vb[lax.rem(y - owner // NZ + NY, NY)]
+    for j, (low_step, high_step) in enumerate(((0, 4), (1, 3), (-1, -3), (2, -2))):
+        target = at(y, z - jnp.where(upper == 1, high_step, low_step))
+        if j == 0:
+            @pl.when(upper == 0)
+            def _():
+                vc[0] = vsrc[...]
+
+            @pl.when(upper == 1)
+            def _(target=target):
+                push(vsrc, vc.at[0], s_vc, r_vc, target, h)
+        else:
+            push(vsrc, vc.at[j], s_vc, r_vc, target, h)
 
     for where in range(2):
         wait_for(qbuf.at[pl.ds(where * 2, 2)], r_q.at[where])
@@ -223,9 +244,6 @@
             q2[r * 2 + g // 4, pl.ds((g % 4) * BLK, BLK), :] = qbuf[
                 source_block[r], :, pl.ds(g * HD, HD)
             ]
-
-    send_z(3)
-    send_z(5)
 
     def attend_rows(r, load, size, dz):
         tiles = (2 * r, 2 * r + 1)
@@ -275,32 +293,32 @@
             wait_for(kv.at[dz], r_z.at[dz])
         return load, 8 * BLK, dz
 
-    attend(*chunk(1))
-
-    near = lax.rem(z - lax.rem(owner, NZ) + NZ, NZ)
-    wait_for(vb.at[pl.ds(1, NZ - 1)], r_vb)
-    index = lax.rem(y, 4)
-    vc[index] = vb[near]
-    for t in range(1, 4):
-        push(
-            vc.at[index], vc.at[index], s_vc, r_vc,
-            at((y // 4) * 4 + lax.rem(index + t, 4), z), h,
-        )
-    send_z(4)
-
-    attend(*chunk(7))
+    attend(*chunk(4))
+    send_z(1)
+    send_z(7)
+    attend(*chunk(3))
+    attend(*chunk(5))
     attend(*chunk(0))
     attend(*chunk(2))
     attend(*chunk(6))
-    wait_for(vc.at[pl.ds(0, 3)], r_vc)
+
+    def wait_vertical(sem):
+        @pl.when(upper == 0)
+        def _():
+            wait_for(vc.at[pl.ds(0, 3)], sem)
+
+        @pl.when(upper == 1)
+        def _():
+            wait_for(vc, sem)
+
+    wait_vertical(r_vc)
     attend(
         lambda: (vc[:, 0].reshape(4 * BLK, HD), vc[:, 1].reshape(4 * BLK, HD)), 4 * BLK, None
     )
-    attend(*chunk(3))
-    attend(*chunk(5))
-    last_chunk = chunk(4)
+    last_chunks = chunk(1), chunk(7)
 
     lanes = lax.broadcasted_iota(jnp.int32, (BLK, 128), 1)
+    spot = lax.broadcasted_iota(jnp.int32, (BLK, 128), 0) & (TOK - 1)
 
     def finish(r):
         stats = jnp.zeros((BLK, 128), jnp.float32)
@@ -309,38 +327,42 @@
             total = jnp.sum(ls[i], axis=1, keepdims=True)
             mixed = acc[i] / total
             weight = mx[i] * SCALE2 + jnp.log(total) * LOG2E
-            big = weight.astype(jnp.bfloat16).astype(jnp.float32)
-            rest = weight - big
-            mid = rest.astype(jnp.bfloat16).astype(jnp.float32)
-            tail = rest - mid
             for j in range(4):
                 g = half * 4 + j
                 rows = slice(j * BLK, (j + 1) * BLK)
                 ostage[r, :, g * HD:(g + 1) * HD] = mixed[rows].astype(jnp.bfloat16)
-                stats = jnp.where(lanes == g, big[rows], stats)
-                stats = jnp.where(lanes == QH + g, mid[rows], stats)
-                stats = jnp.where(lanes == 2 * QH + g, tail[rows], stats)
-        ostage[r, :, WIDTH:STAT] = stats.astype(jnp.bfloat16)
-
-    for r in (0, 2, 1, 3):
-        attend_rows(r, *last_chunk)
+                stats = jnp.where(lanes == g * TOK + spot, weight[rows], stats)
+        for t in range(4):
+            lstage[r, t] = jnp.sum(stats[t * TOK:(t + 1) * TOK], axis=0, keepdims=True)
+
+    for i in range(4):
+        r = (i % 2) * 2 + ((i // 2) ^ ((h // 2) & 1))
+        home = homes[i % 2]
+        for last in last_chunks:
+            attend_rows(r, *last)
         finish(r)
-        for t in range(4):
+        for k in range(4):
+            t = lax.rem(h + k, 4)
+            token_device = lax.rem(r, 2) * 4 + t
             push(
-                ostage.at[r, pl.ds(t * TOK, TOK), :], orecv.at[r // 2, h],
-                s_out, r_out.at[h], homes[r // 2], (r % 2) * 4 + t,
+                ostage.at[r, pl.ds(pl.multiple_of(t * TOK, TOK), TOK), :], orecv.at[i % 2, h],
+                s_out, r_out.at[h], home, token_device,
+            )
+            push(
+                lstage.at[r, t], lrecv.at[i % 2, h], s_stat, r_stat.at[h],
+                home, token_device,
             )
 
     for head in range(NKV):
         wait_for(orecv.at[:, head], r_out.at[head])
-        logs = []
-        for i in range(2):
-            terms = orecv[i, head, :, WIDTH:STAT].astype(jnp.float32)
-            logs.append(terms + pltpu.roll(terms, 128 - QH, 1) + pltpu.roll(terms, 128 - 2 * QH, 1))
-        share = 1.0 / (1.0 + jnp.exp2(logs[1] - logs[0]))
+        wait_for(lrecv.at[:, head], r_stat.at[head])
+        share = 1.0 / (1.0 + jnp.exp2(lrecv[1, head] - lrecv[0, head]))
+        share = jnp.broadcast_to(share, (TOK, 128))
         for g in range(QH):
             cols = slice(g * HD, (g + 1) * HD)
-            part = share[:, g:g + 1]
+            part = jnp.sum(
+                jnp.where(lanes[:TOK] == g * TOK + spot[:TOK], share, 0.0), axis=1, keepdims=True
+            )
             one = orecv[0, head, :, cols].astype(jnp.float32)
             two = orecv[1, head, :, cols].astype(jnp.float32)
             out_ref[:, head * WIDTH + g * HD:head * WIDTH + (g + 1) * HD] = (
@@ -353,12 +375,13 @@
         wait_for(qbuf.at[pl.ds(where * 2, 2)], s_q.at[where])
     wait_for(va.at[pl.ds(1, NY - 1)], s_va)
     wait_for(vb.at[pl.ds(1, NZ - 1)], s_vb)
-    wait_for(vc.at[pl.ds(0, 3)], s_vc)
+    wait_vertical(s_vc)
     for dz in range(NZ):
         wait_for(gath.at[dz], s_y.at[dz])
     for dz in range(1, NZ):
         wait_for(stag.at[dz], s_z.at[dz])
     wait_for(ostage, s_out)
+    wait_for(lstage, s_stat)
 
 
 def per_device(queries, keys, values, vertical, slash_blocks, slash_count, row_order):
@@ -389,16 +412,19 @@
             vmem((NZ, 8, 2, BLK, HD), bf16),
             vmem((NY, 2, BLK, HD), bf16),
             vmem((NZ, 2, BLK, HD), bf16),
+            vmem((2, BLK, HD), bf16),
             vmem((4, 2, BLK, HD), bf16),
             vmem((8, 256, HD), f32),
             vmem((8, 256, 128), f32),
             vmem((8, 256, 128), f32),
             vmem((4, NZ, 8 * BLK), f32),
-            vmem((4, BLK, STAT), bf16),
-            vmem((2, NKV, TOK, STAT), bf16),
+            vmem((4, BLK, WIDTH), bf16),
+            vmem((2, NKV, TOK, WIDTH), bf16),
+            vmem((4, 4, 1, 128), f32),
+            vmem((2, NKV, 1, 128), f32),
             dma((5,)),
-            dma((2,)), dma((2,)), dma, dma, dma, dma((NZ,)), dma((NZ,)), dma,
-            dma((2,)), dma((2,)), dma, dma, dma, dma((NZ,)), dma((NZ,)), dma((NKV,)),
+            dma((2,)), dma((2,)), dma, dma, dma, dma((NZ,)), dma((NZ,)), dma, dma,
+            dma((2,)), dma((2,)), dma, dma, dma, dma((NZ,)), dma((NZ,)), dma((NKV,)), dma((NKV,)),
         ],
         compiler_params=pltpu.CompilerParams(
             collective_id=0, has_side_effects=True, vmem_limit_bytes=60 * 1024 * 1024

time: 111 us -> 96.8 us (0.87)
  the two profiles are of different devices: /device:TPU:87 before, /device:TPU:1 now
where the time goes in v3:
time: 96.8 us; the launch traced here: 96.6 us
  Pallas kernels  94.9 us (98%)
  local copies, waits for them, and re-layouts  1.67 us (2%)
    pallas_call x1, Pallas kernels, per_device(): pl.pallas_call(kernel, out_shape=jax.ShapeDtypeStruct(queries.shape, bf16...  94.9 us

profile of v3, /device:TPU:1, one launch (start us, length us, event | category | flops | bytes accessed | tf_op | source)
XLA Modules:
  0.0 96.6 jit_solution(5053720555292846320)
XLA Ops:
  0.0 94.9 %shard_map.73 = bf16[16,8192]{1,0:T(8,128)(2,1)} custom-call(bf16[16,8192]{1,0:T(8,128)(2,1)} %q_ref.1, bf16[32,64,128]{2,1,0:T(8,128)(2,1)} %bitcast.2, bf16[32,64,128]{2,1,0:T(8,128)(2,1)} %bitcast.3, s32[1,8]{1,0:T(1,128)} %vert_ref.1, s32[1,2,32]{2,1,0:T(2,128)} %lists_ref.1, s32[1,2]{1,0:T(1,128)} %cnt_ref.1, s32[1,2]{1,0:T(1,128)} %ord_ref.1), custom_call_target="tpu_custom_call" | custom-call | tf_op jit(solution)/shard_map/pallas_call | solution.py:395
  95.0 1.7 %copy.9 = bf16[16,8192]{1,0:T(8,128)(2,1)} copy(bf16[16,8192]{1,0:T(8,128)(2,1)} %shard_map.73) | data formatting | bytes 524288

commit v4 on v3

--- a/solution.py
+++ b/solution.py
@@ -21,7 +21,7 @@
 NEG = -1e30
 SCALE2 = math.log2(math.e) / math.sqrt(HD)
 LOG2E = math.log2(math.e)
-ROUTES = ((0, 0, 2, (0, 1)), (-1, 2, 2, (0, 1)), (1, 4, 2, (0, 1)), (-2, 6, 1, (0,)), (2, 7, 1, (1,)))
+ROUTES = ((-1, 2, 2, (0, 1)), (1, 4, 2, (0, 1)), (-2, 6, 1, (0,)), (2, 7, 1, (1,)))
 
 
 def wait_for(ref, sem):
@@ -29,10 +29,11 @@
 
 
 def kernel(
-    q_ref, k_ref, v_ref, vert_ref, lists_ref, cnt_ref, ord_ref, out_ref,
+    q_ref, k_ref, v_ref, vert_hbm, lists_hbm, cnt_hbm, ord_hbm, out_ref,
+    vert_ref, lists_ref, cnt_ref, ord_ref,
     kbuf, vbuf, mrow, mall, msm, pickv, picks, qbuf, q2, gath, stag, kv, va, vb, vsrc, vc,
     acc, mx, ls, bias, ostage, orecv, lstage, lrecv,
-    lsem, s_meta, s_q, s_va, s_vb, s_vc, s_y, s_z, s_out, s_stat,
+    lsem, ssem, s_meta, s_q, s_va, s_vb, s_vc, s_y, s_z, s_out, s_stat,
     r_meta, r_q, r_va, r_vb, r_vc, r_y, r_z, r_out, r_stat,
 ):
     me = lax.axis_index("ctx")
@@ -48,10 +49,16 @@
             device_id=(ctx, kvh), device_id_type=MESH,
         ).start()
 
+    small = [
+        pltpu.make_async_copy(src, dst, ssem.at[i])
+        for i, (src, dst) in enumerate((
+            (vert_hbm, vert_ref), (lists_hbm, lists_ref), (cnt_hbm, cnt_ref), (ord_hbm, ord_ref),
+        ))
+    ]
+    for copy in small:
+        copy.start()
     load_k = pltpu.make_async_copy(k_ref, kbuf, lsem.at[0])
     load_v = pltpu.make_async_copy(v_ref, vbuf, lsem.at[1])
-    load_k.start()
-    load_v.start()
 
     homes = (at(y + 2, z), at(y - 2, z))
 
@@ -66,6 +73,10 @@
                 barrier, inc=1, device_id=(home, lax.rem(h + t, NKV)), device_id_type=MESH
             )
 
+    for copy in small:
+        copy.wait()
+    load_k.start()
+    load_v.start()
     lane = lax.broadcasted_iota(jnp.int32, (1, 128), 1)
     mrow[0] = jnp.full((1, 128), -1, jnp.int32)
     mrow[0, :, 0:SMAX] = lists_ref[0, 0:1, :]
@@ -75,12 +86,13 @@
     row = jnp.where(lane < limit, row, -1)
     row = jnp.where(lane == 2 * SMAX, ord_ref[0, 0], row)
     row = jnp.where(lane == 2 * SMAX + 1, ord_ref[0, 1], row)
-    mall[me] = row
+    spot_of_me = z * NY + y
+    mall[spot_of_me] = row
 
     pl.semaphore_wait(barrier, NZ - 1 + NY - 1 + 2 * (NKV - 1))
 
-    for t in range(1, NZ):
-        push(mall.at[me], mall.at[me], s_meta.at[0], r_meta.at[0], at(y, z + t), h)
+    for t in range(1, NY):
+        push(mall.at[spot_of_me], mall.at[spot_of_me], s_meta.at[0], r_meta.at[0], at(y + t, z), h)
 
     token_rows = pl.ds(pl.multiple_of(lax.rem(h, 4) * TOK, TOK), TOK)
 
@@ -93,10 +105,13 @@
                 s_q.at[where], r_q.at[where], homes[1 - where], t,
             )
 
-    wait_for(mall.at[pl.ds(0, NZ - 1)], r_meta.at[0])
-    my_row = pl.ds(pl.multiple_of(y * NZ, NZ), NZ)
-    for t in range(1, NY):
-        push(mall.at[my_row], mall.at[my_row], s_meta.at[1], r_meta.at[1], at(y + t, z), h)
+    send_queries(0)
+    send_queries(1)
+
+    wait_for(mall.at[pl.ds(0, NY - 1)], r_meta.at[0])
+    column = pl.ds(pl.multiple_of(z * NY, NY), NY)
+    for t in range(1, NZ):
+        push(mall.at[column], mall.at[column], s_meta.at[1], r_meta.at[1], at(y, z + t), h)
 
     load_k.wait()
     load_v.wait()
@@ -109,14 +124,15 @@
     for b in range(1, NZ):
         push(va.at[0], va.at[b], s_va, r_va, at(y, z + b), h)
 
-    wait_for(mall.at[pl.ds(0, NCTX - NZ)], r_meta.at[1])
+    wait_for(mall.at[pl.ds(0, NCTX - NY)], r_meta.at[1])
     to_msm = [
-        pltpu.make_async_copy(mall.at[homes[i]], msm.at[i], lsem.at[3 + i]) for i in range(2)
+        pltpu.make_async_copy(mall.at[z * NY + homes[i] // NZ], msm.at[i], lsem.at[3 + i]) for i in range(2)
     ]
     for copy in to_msm:
         copy.start()
-    low = mall[0:NCTX // 2].reshape(NCTX // 2, 128)
-    high = mall[NCTX // 2:NCTX].reshape(NCTX // 2, 128)
+    half = NY // 2
+    low = jnp.concatenate([mall[i * NY:i * NY + half].reshape(half, 128) for i in range(NZ)])
+    high = jnp.concatenate([mall[i * NY + half:(i + 1) * NY].reshape(half, 128) for i in range(NZ)])
     wide = lax.broadcasted_iota(jnp.int32, (NCTX // 2, 128), 1)
     entries = jnp.where(wide < 2 * SMAX, low, pltpu.roll(high, 2 * SMAX, 1))
     own = lax.shift_right_arithmetic(entries, 5) == me
@@ -124,32 +140,36 @@
     first = jnp.min(jnp.where(own, local, 99), axis=1, keepdims=True)
     last = jnp.max(jnp.where(own, local, 0), axis=1, keepdims=True)
     first = jnp.where(first == 99, 0, first)
-    pickv[...] = jnp.where(wide == 0, first, last)
+    tall = lax.broadcasted_iota(jnp.int32, (NCTX // 2, 128), 0)
+    pickv[0] = jnp.sum(jnp.where(wide == tall, first + 32 * last, 0), axis=0, keepdims=True)
     to_picks = pltpu.make_async_copy(pickv, picks, lsem.at[2])
     to_picks.start()
     to_picks.wait()
 
+    def stage(ref, dz, slot, dy, which):
+        pair = lax.rem(z + dz, NZ) * 4 + lax.rem(y + dy + 2 + NY, 4)
+        both = picks[0, 0, pair]
+        pick = both & 31 if which == 0 else lax.shift_right_logical(both, 5)
+        ref[dz, slot, 0] = kbuf[pick]
+        ref[dz, slot, 1] = vbuf[pick]
+
+    def send_own(dz):
+        for i in range(2):
+            stage(stag, dz, i, 0, i)
+        if dz != 0:
+            push(
+                stag.at[dz, pl.ds(0, 2)], kv.at[dz, pl.ds(0, 2)],
+                s_z.at[dz], r_z.at[dz], at(y, z + dz), h,
+            )
+
     def send_y(dz):
         for dy, start, count, which in ROUTES:
-            pair = lax.rem(y + dy + 2 + NY, 4) * NZ + lax.rem(z + dz, NZ)
             for i in range(count):
-                pick = picks[pair, which[i]]
-                if dy == 0:
-                    stag[dz, start + i, 0] = kbuf[pick]
-                    stag[dz, start + i, 1] = vbuf[pick]
-                else:
-                    gath[dz, start + i - 2, 0] = kbuf[pick]
-                    gath[dz, start + i - 2, 1] = vbuf[pick]
-            if dy == 0 and dz != 0:
-                push(
-                    stag.at[dz, pl.ds(0, 2)], kv.at[dz, pl.ds(0, 2)],
-                    s_z.at[dz], r_z.at[dz], at(y, z + dz), h,
-                )
-            if dy != 0:
-                push(
-                    gath.at[dz, pl.ds(start - 2, count)], stag.at[dz, pl.ds(start, count)],
-                    s_y.at[dz], r_y.at[dz], at(y + dy, z), h,
-                )
+                stage(gath, dz, start + i - 2, dy, which[i])
+            push(
+                gath.at[dz, pl.ds(start - 2, count)], stag.at[dz, pl.ds(start, count)],
+                s_y.at[dz], r_y.at[dz], at(y + dy, z), h,
+            )
 
     def send_z(dz):
         wait_for(stag.at[dz, pl.ds(2, 6)], r_y.at[dz])
@@ -158,13 +178,13 @@
             s_z.at[dz], r_z.at[dz], at(y, z + dz), h,
         )
 
-    for dz in (4, 3, 5):
+    for dz in (1,):
         send_y(dz)
-    send_queries(0)
-    send_queries(1)
-    for dz in (2, 6):
+    for dz in (1, 7, 2, 6, 3, 5, 4, 0,):
+        send_own(dz)
+    for dz in (7, 2, 6, 3, 5,):
         send_y(dz)
-    for dz in (4, 3, 5):
+    for dz in (1, 7, 2, 6,):
         send_z(dz)
 
     owner = vert_ref[0, z] // 32
@@ -173,7 +193,7 @@
     for a in range(1, NY):
         push(vb.at[0], vb.at[a], s_vb, r_vb, at(y + a, z), h)
 
-    for dz in (1, 7, 0):
+    for dz in (4, 0,):
         send_y(dz)
 
     for copy in to_msm:
@@ -218,13 +238,13 @@
         ls[i] = jnp.zeros((256, 128), jnp.float32)
         mx[i] = jnp.full((256, 128), NEG, jnp.float32)
 
-    send_z(2)
-    send_z(6)
+    for dz in (3, 5,):
+        send_z(dz)
 
     upper = y // 4
     wait_for(vb.at[pl.ds(1, NY - 1)], r_vb)
     vsrc[...] = vb[lax.rem(y - owner // NZ + NY, NY)]
-    for j, (low_step, high_step) in enumerate(((0, 4), (1, 3), (-1, -3), (2, -2))):
+    for j, (low_step, high_step) in enumerate(((0, 1), (4, -1), (2, 3), (-2, -3))):
         target = at(y, z - jnp.where(upper == 1, high_step, low_step))
         if j == 0:
             @pl.when(upper == 0)
@@ -293,14 +313,15 @@
             wait_for(kv.at[dz], r_z.at[dz])
         return load, 8 * BLK, dz
 
-    attend(*chunk(4))
-    send_z(1)
-    send_z(7)
+    attend(*chunk(1))
+    for dz in (4,):
+        send_z(dz)
+    attend(*chunk(7))
+    attend(*chunk(2))
+    attend(*chunk(6))
+    attend(*chunk(0))
     attend(*chunk(3))
     attend(*chunk(5))
-    attend(*chunk(0))
-    attend(*chunk(2))
-    attend(*chunk(6))
 
     def wait_vertical(sem):
         @pl.when(upper == 0)
@@ -315,7 +336,7 @@
     attend(
         lambda: (vc[:, 0].reshape(4 * BLK, HD), vc[:, 1].reshape(4 * BLK, HD)), 4 * BLK, None
     )
-    last_chunks = chunk(1), chunk(7)
+    last_chunks = (chunk(4),)
 
     lanes = lax.broadcasted_iota(jnp.int32, (BLK, 128), 1)
     spot = lax.broadcasted_iota(jnp.int32, (BLK, 128), 0) & (TOK - 1)
@@ -369,8 +390,8 @@
                 one * part + two * (1.0 - part)
             ).astype(jnp.bfloat16)
 
-    wait_for(mall.at[pl.ds(0, NZ - 1)], s_meta.at[0])
-    wait_for(mall.at[pl.ds(0, NCTX - NZ)], s_meta.at[1])
+    wait_for(mall.at[pl.ds(0, NY - 1)], s_meta.at[0])
+    wait_for(mall.at[pl.ds(0, NCTX - NY)], s_meta.at[1])
     for where in range(2):
         wait_for(qbuf.at[pl.ds(where * 2, 2)], s_q.at[where])
     wait_for(va.at[pl.ds(1, NY - 1)], s_va)
@@ -391,20 +412,23 @@
     dma = pltpu.SemaphoreType.DMA
     hbm_spec = pl.BlockSpec(memory_space=pltpu.HBM)
     vmem_spec = pl.BlockSpec(memory_space=pltpu.VMEM)
-    smem_spec = pl.BlockSpec(memory_space=pltpu.SMEM)
     return pl.pallas_call(
         kernel,
         out_shape=jax.ShapeDtypeStruct(queries.shape, bf16),
-        in_specs=[hbm_spec, hbm_spec, hbm_spec, smem_spec, vmem_spec, smem_spec, smem_spec],
+        in_specs=[hbm_spec] * 7,
         out_specs=vmem_spec,
         scratch_shapes=[
+            pltpu.SMEM((1, 8), i32),
+            vmem((1, 2, SMAX), i32),
+            pltpu.SMEM((1, 2), i32),
+            pltpu.SMEM((1, 2), i32),
             vmem((blocks, BLK, HD), bf16),
             vmem((blocks, BLK, HD), bf16),
             vmem((1, 1, 128), i32),
             vmem((NCTX, 1, 128), i32),
             pltpu.SMEM((2, 1, 128), i32),
-            vmem((NCTX // 2, 128), i32),
-            pltpu.SMEM((NCTX // 2, 128), i32),
+            vmem((1, 1, 128), i32),
+            pltpu.SMEM((1, 1, 128), i32),
             vmem((4, BLK, WIDTH), bf16),
             vmem((8, 256, HD), bf16),
             vmem((NZ, 6, 2, BLK, HD), bf16),
@@ -423,11 +447,12 @@
             vmem((4, 4, 1, 128), f32),
             vmem((2, NKV, 1, 128), f32),
             dma((5,)),
+            dma((4,)),
             dma((2,)), dma((2,)), dma, dma, dma, dma((NZ,)), dma((NZ,)), dma, dma,
             dma((2,)), dma((2,)), dma, dma, dma, dma((NZ,)), dma((NZ,)), dma((NKV,)), dma((NKV,)),
         ],
         compiler_params=pltpu.CompilerParams(
-            collective_id=0, has_side_effects=True, vmem_limit_bytes=60 * 1024 * 1024
+            collective_id=0, has_side_effects=True, vmem_limit_bytes=int(53.6 * 1024 * 1024)
         ),
     )(
         queries,

time: 96.8 us -> 92.2 us (0.952)
  Pallas kernels: 94.9 us -> 89.7 us
    pallas_call x1, Pallas kernels: 94.9 us -> 89.7 us  [per_device(): pl.pallas_call(kernel, out_shape=jax.ShapeDtypeStruct(queries.shape, bf16...]
where the time goes in v4:
time: 92.2 us; the launch traced here: 91.1 us
  Pallas kernels  89.7 us (97%)
  local copies, waits for them, and re-layouts  1.4 us (2%)
    pallas_call x1, Pallas kernels, per_device(): pl.pallas_call(kernel, out_shape=jax.ShapeDtypeStruct(queries.shape, bf16...  89.7 us

profile of v4, /device:TPU:1, one launch (start us, length us, event | category | flops | bytes accessed | tf_op | source)
XLA Modules:
  0.0 91.1 jit_solution(9136128936631429326)
XLA Ops:
  0.0 0.0 copy-start.2
  0.0 0.0 copy-start.3
  0.0 0.0 copy-start
  0.0 0.0 copy-start.1
  0.0 0.6 copy-done.2
  0.7 0.0 copy-done.3
  0.7 0.0 copy-done
  0.7 0.0 copy-done.1
  0.7 89.7 %shard_map.73 = bf16[16,8192]{1,0:T(8,128)(2,1)S(1)} custom-call(bf16[16,8192]{1,0:T(8,128)(2,1)} %q_ref.1, bf16[32,64,128]{2,1,0:T(8,128)(2,1)} %bitcast.2, bf16[32,64,128]{2,1,0:T(8,128)(2,1)} %bitcast.3, s32[1,8]{1,0:T(1,128)S(1)} %copy-done.1, s32[1,2,32]{2,1,0:T(2,128)S(1)} %copy-done, s32[1,2]{1,0:T(1,128)S(1)} %copy-done.2, s32[1,2]{1,0:T(1,128)S(1)} %copy-done.3), custom_call_target="tpu_custom_call" | custom-call | tf_op jit(solution)/shard_map/pallas_call | solution.py:415
  90.4 0.7 copy.9
Async XLA Ops:
  0.0 0.7 copy-start.2
  0.0 0.7 copy-start.3
  0.0 0.7 copy-start
  0.0 0.7 copy-start.1

commit v5 on v4

--- a/solution.py
+++ b/solution.py
@@ -366,15 +366,19 @@
             t = lax.rem(h + k, 4)
             token_device = lax.rem(r, 2) * 4 + t
             push(
+                lstage.at[r, t], lrecv.at[i % 2, h], s_stat, r_stat.at[h],
+                home, token_device,
+            )
+        for k in range(4):
+            t = lax.rem(h + k, 4)
+            token_device = lax.rem(r, 2) * 4 + t
+            push(
                 ostage.at[r, pl.ds(pl.multiple_of(t * TOK, TOK), TOK), :], orecv.at[i % 2, h],
                 s_out, r_out.at[h], home, token_device,
             )
-            push(
-                lstage.at[r, t], lrecv.at[i % 2, h], s_stat, r_stat.at[h],
-                home, token_device,
-            )
-
-    for head in range(NKV):
+
+    def merge(i, _):
+        head = lax.rem(h + i, NKV)
         wait_for(orecv.at[:, head], r_out.at[head])
         wait_for(lrecv.at[:, head], r_stat.at[head])
         share = 1.0 / (1.0 + jnp.exp2(lrecv[1, head] - lrecv[0, head]))
@@ -386,9 +390,13 @@
             )
             one = orecv[0, head, :, cols].astype(jnp.float32)
             two = orecv[1, head, :, cols].astype(jnp.float32)
-            out_ref[:, head * WIDTH + g * HD:head * WIDTH + (g + 1) * HD] = (
+            spread = pl.ds(pl.multiple_of(head * WIDTH + g * HD, HD), HD)
+            out_ref[:, spread] = (
                 one * part + two * (1.0 - part)
             ).astype(jnp.bfloat16)
+        return 0
+
+    lax.fori_loop(0, NKV, merge, 0)
 
     wait_for(mall.at[pl.ds(0, NY - 1)], s_meta.at[0])
     wait_for(mall.at[pl.ds(0, NCTX - NY)], s_meta.at[1])
@@ -452,7 +460,7 @@
             dma((2,)), dma((2,)), dma, dma, dma, dma((NZ,)), dma((NZ,)), dma((NKV,)), dma((NKV,)),
         ],
         compiler_params=pltpu.CompilerParams(
-            collective_id=0, has_side_effects=True, vmem_limit_bytes=int(53.6 * 1024 * 1024)
+            collective_id=0, has_side_effects=True, vmem_limit_bytes=int(53.67 * 1024 * 1024)
         ),
     )(
         queries,

time: 92.2 us -> 92.1 us (level)
  no operation moved by 1% of the time
where the time goes in v5:
time: 92.1 us; the launch traced here: 91.2 us
  Pallas kernels  89.8 us (98%)
  local copies, waits for them, and re-layouts  1.4 us (2%)
    pallas_call x1, Pallas kernels, per_device(): pl.pallas_call(kernel, out_shape=jax.ShapeDtypeStruct(queries.shape, bf16...  89.8 us

profile of v5, /device:TPU:1, one launch (start us, length us, event | category | flops | bytes accessed | tf_op | source)
XLA Modules:
  0.0 91.2 jit_solution(9318887142216683625)
XLA Ops:
  0.0 0.0 copy-start.2
  0.0 0.0 copy-start.3
  0.0 0.0 copy-start
  0.0 0.0 copy-start.1
  0.0 0.6 copy-done.2
  0.7 0.0 copy-done.3
  0.7 0.0 copy-done
  0.7 0.0 copy-done.1
  0.7 89.8 %shard_map.73 = bf16[16,8192]{1,0:T(8,128)(2,1)S(1)} custom-call(bf16[16,8192]{1,0:T(8,128)(2,1)} %q_ref.1, bf16[32,64,128]{2,1,0:T(8,128)(2,1)} %bitcast.2, bf16[32,64,128]{2,1,0:T(8,128)(2,1)} %bitcast.3, s32[1,8]{1,0:T(1,128)S(1)} %copy-done.1, s32[1,2,32]{2,1,0:T(2,128)S(1)} %copy-done, s32[1,2]{1,0:T(1,128)S(1)} %copy-done.2, s32[1,2]{1,0:T(1,128)S(1)} %copy-done.3), custom_call_target="tpu_custom_call" | custom-call | tf_op jit(solution)/shard_map/pallas_call | solution.py:423
  90.5 0.7 copy.9
Async XLA Ops:
  0.0 0.7 copy-start.2
  0.0 0.7 copy-start.3
  0.0 0.7 copy-start
  0.0 0.7 copy-start.1
